TPU v7x, 256 devices: a whole 4x4x8 slice. The times are simulated.
256 devices in a mesh: slab: 32 (over y, x, z_lo), blk: 8 (over z_hi, core).
Axes of the slice: x: 4, y: 4, z: 8 (z_hi: 4, z_lo: 2; z = z_hi * 2 + z_lo), core: 2. Of those that a mesh axis runs over, the one named last changes fastest.
Arguments:
- interior: float32 [64, 512, 512], P('slab', 'blk'), may hold values from -6 to 6
- sources: float32 [64, 512, 512], P('slab', 'blk'), may hold values from -12 to 12
- absorption: float32 [64, 512, 512], P('slab', 'blk'), may hold values from 0.1 to 4
- bem_panel: bfloat16 [8192, 131072], P('blk', 'slab'), may hold values from -0.03125 to 0.03125
- incident: bfloat16 [131072, 512], P('slab'), may hold values from -160 to 160
- node_cell: int32 [131072], P('slab'), may hold values from 0 to 255
- offset: int32 [1], replicated, may hold values from 0 to 122880, as said below
Outputs:
- relaxed: float32 [64, 512, 512], P('slab', 'blk')
- boundary_flux: float32 [8192, 512], P(('blk', 'slab'))
Inputs may be any that keep to these rules, and one draw needn't show every extreme that they name: offset is a multiple of 8192; rows offset to offset + 8191 lie among the 131072 boundary nodes.
All inputs are finite; a program needn't handle non-finite values.
Results may differ from a plain program's by a relative error of at most 0.0034.
Values sent between devices are 32-bit elements; how exact they have to be, the bound alone decides.
A program may use at most 64 MiB of HBM per device.

v0:
```python
import jax
import jax.numpy as jnp
from jax import lax
from jax.sharding import PartitionSpec as P

SWEEPS = 2


omega = 0.6
center_weight = 8.0 / 3.0


def padded_2(cells, sides, width):
    for axis, dim in sides:
        count = lax.axis_size(axis)
        ends = count - 1
        head = lax.slice_in_dim(cells, 0, width, axis=dim)
        tail = lax.slice_in_dim(cells, cells.shape[dim] - width, cells.shape[dim], axis=dim)
        cells = jnp.concatenate(
            [
                lax.ppermute(tail, axis, [(i, (i + 1) % count) for i in range(ends)]),
                cells,
                lax.ppermute(head, axis, [((i + 1) % count, i) for i in range(ends)]),
            ],
            axis=dim,
        )
    return cells


def stiffness(padded):
    along_x = padded[:, :, :-2] + padded[:, :, 2:]
    middle = padded[:, :, 1:-1]
    plus_mid = along_x + middle
    plane_sum = plus_mid[:, :-2] + plus_mid[:, 1:-1] + plus_mid[:, 2:]
    total_sum = plane_sum[:-2] + plane_sum[1:-1] + plane_sum[2:]
    cross_xy = along_x[:, :-2] + along_x[:, 2:]
    corner_sum = cross_xy[:-2] + cross_xy[2:]
    face_sum = (
        along_x[1:-1, 1:-1]
        + middle[1:-1, :-2]
        + middle[1:-1, 2:]
        + middle[:-2, 1:-1]
        + middle[2:, 1:-1]
    )
    center = middle[1:-1, 1:-1]
    edge_sum = total_sum - center - face_sum - corner_sum
    return center_weight * center - edge_sum / 6.0 - corner_sum / 12.0


def sweep_once(padded, sources, absorption):
    center = padded[1:-1, 1:-1, 1:-1]
    applied = stiffness(padded) + absorption * center
    return center + omega * (sources - applied) / (center_weight + absorption)


def pad_x(values):
    return jnp.pad(values, ((0, 0), (0, 0), (1, 1)))


def per_device(interior, sources, absorption, bem_panel, incident, node_cell, offset):
    depth_z, depth_y, width_x = interior.shape
    current = interior
    for sweep_idx in range(SWEEPS):
        padded = padded_2(current, (("slab", 0), ("blk", 1)), 1)
        current = sweep_once(pad_x(padded), sources, absorption)
    slab_cols = incident.shape[0]
    own_count = slab_cols // lax.axis_size("blk")
    x_faces = jnp.stack([interior[:, :, 0], interior[:, :, width_x - 1]], axis=-1).reshape(-1)
    own_cells = lax.dynamic_slice_in_dim(node_cell, lax.axis_index("blk") * own_count, own_count, 0)
    own_trace = jnp.take(x_faces, own_cells, axis=0)
    trace = lax.all_gather(own_trace, "blk", axis=0, tiled=True)
    fields = (incident.astype(jnp.float32) + trace[:, None]).astype(jnp.bfloat16)
    wide = fields.astype(jnp.float32)
    node_total = slab_cols * lax.axis_size("slab")
    squares = lax.psum(jnp.sum(wide * wide, axis=0), "slab")
    norms = jnp.sqrt(squares / node_total + 1e-06)
    panel_rows = bem_panel.shape[0]
    first_col = lax.axis_index("slab") * slab_cols
    shift_rows = offset[0] + lax.axis_index("blk") * panel_rows - first_col
    share = panel_rows // lax.axis_size("slab")
    product = jnp.dot(bem_panel, fields, preferred_element_type=jnp.float32)
    node_pos = shift_rows + jnp.arange(panel_rows, dtype=jnp.int32)
    valid = (node_pos >= 0) & (node_pos < slab_cols)
    picked = jnp.take(wide, jnp.clip(node_pos, 0, slab_cols - 1), axis=0)
    summed = product + 0.5 * jnp.where(valid[:, None], picked, 0.0)
    summed = summed / norms[None, :]
    summed_all = lax.psum(summed, "slab")
    owned = lax.dynamic_slice_in_dim(summed_all, lax.axis_index("slab") * share, share, 0)
    return (current, owned)


def solution(mesh):
    in_specs = (
        P("slab", "blk", None),
        P("slab", "blk", None),
        P("slab", "blk", None),
        P("blk", "slab"),
        P("slab", None),
        P("slab"),
        P(),
    )
    out_specs = (P("slab", "blk", None), P(("blk", "slab"), None))
    return jax.shard_map(
        per_device, mesh=mesh, in_specs=in_specs, out_specs=out_specs, check_vma=False
    )
```

profile of v0, /device:TPU:2, one launch (start us, length us, event | category | flops | bytes accessed | tf_op | source)
XLA Modules:
  0.0 476.1 jit_solution(14701295206737365730)
XLA Ops:
  7.2 1.0 fusion.47
  8.2 3.8 collective-permute-start
  12.0 2.9 collective-permute-start.1
  15.0 1.0 fusion.45
  17.8 3.5 gather_fusion
  21.3 0.8 and_select_fusion
  22.1 18.2 %all-gather = f32[8,1,512]{2,1,0:T(1,128)S(1)} all-gather(f32[1,1,512]{2,1,0:T(1,128)S(1)} %bitcast.13), channel_id=1, replica_groups=mesh['slab'=32,'blk'=8] {'blk'}, dimensions={0}, use_global_device_ids=true | all-gather | bytes 18432 | tf_op jit(solution)/shard_map/all_gather | solution.py:71
  40.3 5.4 %multiply_reduce_fusion = (f32[512]{0:T(512)S(1)}, f32[4096,512]{1,0:T(8,128)}) fusion(f32[4096]{0:T(1024)S(1)} %bitcast.10, bf16[4096,512]{1,0:T(8,128)(2,1)} %param.11), kind=kLoop, calls=%fused_computation.2 | loop fusion | flops 12582400 | bytes 12601344 | tf_op jit(solution)/shard_map/reduce_sum | solution.py:75
  45.7 77.6 %psum.14 = f32[512]{0:T(512)S(1)} all-reduce(f32[512]{0:T(512)S(1)} %get-tuple-element.12), channel_id=1, replica_groups=mesh['slab'=32,'blk'=8] {'slab'}, use_global_device_ids=true, to_apply=%region_1.2 | all-reduce | flops 512 | bytes 4096 | tf_op jit(solution)/shard_map/psum | solution.py:75
  123.3 7.4 %gather_fusion.1 = f32[1024,512]{1,0:T(8,128)S(1)} fusion(f32[4096,512]{1,0:T(8,128)} %get-tuple-element.13, s32[1024]{0:T(1024)S(1)} %get-tuple-element.27), kind=kCustom, calls=%fused_computation.1 | custom fusion | bytes 4198400 | tf_op jit(solution)/shard_map/jit(_take)/gather | solution.py:84
  130.8 1.9 copy.16
  132.8 1.3 collective-permute-start.2
  134.1 1.3 collective-permute-start.3
  135.4 12.0 %fusion = f32[1024,512]{0,1:T(8,128)} fusion(f32[1024,512]{0,1:T(8,128)} %copy.16, bf16[1024,4096]{1,0:T(8,128)(2,1)} %param.10, f32[512]{0:T(512)S(1)} %add_sqrt_fusion, pred[1024]{0:T(1024)(128)(4,1)S(1)} %get-tuple-element.28, pred[1024]{0:T(1024)(128)(4,1)S(1)} %get-tuple-element.29, bf16[4096,512]{1,0:T(8,128)(2,1)} %param.11, f32[4096]{0:T(1024)S(1)} %bitcast.11), kind=kOutput, calls=%fused_computation.5 | convolution fusion | flops 4303880192 | bytes 16797696 | tf_op jit(solution)/shard_map/dot_general | solution.py:81
  148.7 1.9 collective-permute-start.4
  150.6 4.8 %collective-permute-start.5 = (f32[1,64,512]{2,1,0:T(8,128)S(1)}, f32[1,64,512]{2,1,0:T(8,128)S(1)}, u32[]{:S(2)}, u32[]{:S(2)}) collective-permute-start(f32[1,64,512]{2,1,0:T(8,128)S(1)} %get-tuple-element.21), channel_id=1, source_target_pairs={{8,0},{16,8},{24,16},{32,24},{40,32},{48,40},{56,48},{64,56},{72,6... | collective-permute-start | bytes 393224 | tf_op jit(solution)/shard_map/ppermute | solution.py:23
  155.5 1.8 collective-permute-done.4
  157.3 1.8 collective-permute-done.5
  159.1 2.3 collective-permute-start.6
  161.4 1.3 collective-permute-start.7
  162.7 4.3 collective-permute-done.7
  167.6 1.0 fusion.13
  168.7 298.7 %all-reduce.4.cloned.1.call-done = f32[1024,512]{0,1:T(8,128)} async-done(((f32[1024,512]{0,1:T(8,128)}), f32[1024,512]{0,1:T(8,128)}) %all-reduce.4.cloned.1.call-update) | async-done | bytes 2097168 | tf_op jit(solution)/shard_map/psum | solution.py:87
  467.4 1.1 constant_dynamic-slice_fusion
  (38 shorter events, 4.1 us)
Async XLA Ops:
  7.2 460.2 %all-reduce.4.cloned.1.call-start = ((), (), s32[]{:S(2)}) async-start(), calls=%async_computation | async-start | bytes 4194304 | tf_op jit(solution)/shard_map/psum | solution.py:87
  8.2 124.4 %collective-permute-start = (f32[1,64,512]{2,1,0:T(8,128)S(1)}, f32[1,64,512]{2,1,0:T(8,128)S(1)}, u32[]{:S(2)}, u32[]{:S(2)}) collective-permute-start(f32[1,64,512]{2,1,0:T(8,128)S(1)} %get-tuple-element.22), channel_id=1, source_target_pairs={{0,8},{8,16},{16,24},{24,32},{32,40},{40,48},{48,56},{56,64},{64,7... | collective-permute-start | bytes 393224 | tf_op jit(solution)/shard_map/ppermute | solution.py:21
  12.0 120.7 %collective-permute-start.1 = (f32[1,64,512]{2,1,0:T(8,128)S(1)}, f32[1,64,512]{2,1,0:T(8,128)S(1)}, u32[]{:S(2)}, u32[]{:S(2)}) collective-permute-start(f32[1,64,512]{2,1,0:T(8,128)S(1)} %get-tuple-element.23), channel_id=1, source_target_pairs={{8,0},{16,8},{24,16},{32,24},{40,32},{48,40},{56,48},{64,56},{72,6... | collective-permute-start | bytes 393224 | tf_op jit(solution)/shard_map/ppermute | solution.py:23
  130.8 1.9 copy-start
  132.8 14.6 %collective-permute-start.2 = (f32[4,1,512]{2,1,0:T(1,128)S(1)}, f32[4,1,512]{2,1,0:T(1,128)S(1)}, u32[]{:S(2)}, u32[]{:S(2)}) collective-permute-start(f32[4,1,512]{2,1,0:T(1,128)S(1)} %get-tuple-element.16), channel_id=1, source_target_pairs={{0,1},{1,2},{2,3},{3,4},{4,5},{5,6},{6,7},{8,9},{9,10},{10,11},{11... | collective-permute-start | bytes 24584 | tf_op jit(solution)/shard_map/ppermute | solution.py:21
  134.1 13.3 %collective-permute-start.3 = (f32[4,1,512]{2,1,0:T(1,128)S(1)}, f32[4,1,512]{2,1,0:T(1,128)S(1)}, u32[]{:S(2)}, u32[]{:S(2)}) collective-permute-start(f32[4,1,512]{2,1,0:T(1,128)S(1)} %get-tuple-element.17), channel_id=1, source_target_pairs={{1,0},{2,1},{3,2},{4,3},{5,4},{6,5},{7,6},{9,8},{10,9},{11,10},{12... | collective-permute-start | bytes 24584 | tf_op jit(solution)/shard_map/ppermute | solution.py:23
  147.3 0.9 copy-start.1
  147.3 1.0 copy-start.2
  148.7 8.6 %collective-permute-start.4 = (f32[1,64,512]{2,1,0:T(8,128)S(1)}, f32[1,64,512]{2,1,0:T(8,128)S(1)}, u32[]{:S(2)}, u32[]{:S(2)}) collective-permute-start(f32[1,64,512]{2,1,0:T(8,128)S(1)} %get-tuple-element.20), channel_id=1, source_target_pairs={{0,8},{8,16},{16,24},{24,32},{32,40},{40,48},{48,56},{56,64},{64,7... | collective-permute-start | bytes 393224 | tf_op jit(solution)/shard_map/ppermute | solution.py:21
  150.6 8.4 %collective-permute-start.5 = (f32[1,64,512]{2,1,0:T(8,128)S(1)}, f32[1,64,512]{2,1,0:T(8,128)S(1)}, u32[]{:S(2)}, u32[]{:S(2)}) collective-permute-start(f32[1,64,512]{2,1,0:T(8,128)S(1)} %get-tuple-element.21), channel_id=1, source_target_pairs={{8,0},{16,8},{24,16},{32,24},{40,32},{48,40},{56,48},{64,56},{72,6... | collective-permute-start | bytes 393224 | tf_op jit(solution)/shard_map/ppermute | solution.py:23
  159.1 3.6 collective-permute-start.6
  161.4 5.6 %collective-permute-start.7 = (f32[4,1,512]{2,1,0:T(1,128)S(1)}, f32[4,1,512]{2,1,0:T(1,128)S(1)}, u32[]{:S(2)}, u32[]{:S(2)}) collective-permute-start(f32[4,1,512]{2,1,0:T(1,128)S(1)} %get-tuple-element.15), channel_id=1, source_target_pairs={{1,0},{2,1},{3,2},{4,3},{5,4},{6,5},{7,6},{9,8},{10,9},{11,10},{12... | collective-permute-start | bytes 24584 | tf_op jit(solution)/shard_map/ppermute | solution.py:23
Sparse Core Ops, SparseCore 0:
  147.5 319.8 all-reduce.3
where the time goes:
time: 480 us; the launch traced here: 476 us
  waiting for transfers between devices  307 us (64%)
  blocking collectives  95.8 us (20%)
  starting transfers between devices  19.7 us (4%)
  local copies, waits for them, and re-layouts  17.3 us (4%)
  between operations  15 us (3%)
  matrix products  12 us (2%)
  other arithmetic  9.66 us (2%)
    psum x1, waiting for transfers between devices, per_device(): summed_all = lax.psum(summed, 'slab')  299 us
    psum x1, blocking collectives, per_device(): squares = lax.psum(jnp.sum(wide * wide, axis=0), 'slab')  77.6 us
    all_gather x1, blocking collectives, per_device(): trace = lax.all_gather(own_trace, 'blk', axis=0, tiled=True)  18.2 us
    dot_general x1, matrix products, per_device(): product = jnp.dot(bem_panel, fields, preferred_element_type=jnp.float32)  12 us
    ppermute x4, starting transfers between devices, padded_2(): lax.ppermute(head, axis, [((i + 1) % count, i) for i in range(ends)])  10.3 us
  transfers between devices with their start and end apart: 9, of which 4 were waited for; matrix products, arithmetic and copies ran while one was open for 8% of the time, Pallas kernels for 0%

commit v1 on v0

v1 whole, which is shorter than its diff:
```python
import jax
import jax.numpy as jnp
from jax import lax
from jax.experimental import pallas as pl
from jax.experimental.pallas import tpu as pltpu
from jax.sharding import PartitionSpec as P

F32 = jnp.float32
BF16 = jnp.bfloat16
MESH = pl.DeviceIdType.MESH
CENTER = 8.0 / 3.0


def flip(pos, low, high):
    if low:
        pos = pos + 1 - 2 * lax.rem(pos, 2)
    if high:
        pos = 3 - pos
    return pos


XA, XB, YA, YB = ("x", 1, 0), ("x", 0, 1), ("y", 1, 0), ("y", 0, 1)
ORDERS = ((XA, YA, XB, YB), (YA, XA, YB, XB), (XB, YB, XA, YA), (YB, XB, YA, XA))
NODES = 131072.0


def along_x(w, first, last):
    n = w.shape[1]
    left = jnp.where(first, 0.0, pltpu.roll(w, 1, 1))
    right = jnp.where(last, 0.0, pltpu.roll(w, n - 1, 1))
    return left + right


def kernel(
    offset, interior, sources, absorption, bem, incident, cells,
    relaxed, flux,
    pad1, pad2, src, inv, ytx1, ytx2, yrx1, yrx2,
    cell_v, ttx, trx, inc_v, fld, panel,
    prod, rx1, rx2, rx3, rx4, rx5, ntx, nrx,
    load_sem, inc_sem, panel_sem, halo_send, halo_recv,
    trace_send, trace_recv, rs_send, rs_recv, n_send, n_recv,
):
    slab, blk = lax.axis_index("slab"), lax.axis_index("blk")
    my_y, my_x, my_z = slab // 8, lax.rem(slab // 2, 4), lax.rem(slab, 2)

    def at(y, x, z):
        return y * 8 + x * 2 + z

    def toward(dim):
        if dim == "z":
            return (at(my_y, my_x, 1 - my_z), blk)
        axis, low, high = dim
        if axis == "x":
            return (at(my_y, flip(my_x, low, high), my_z), blk)
        return (at(flip(my_y, low, high), my_x, my_z), blk)

    up, down = lax.rem(slab + 1, 32), lax.rem(slab + 31, 32)
    east, west = lax.rem(blk + 1, 8), lax.rem(blk + 7, 8)

    core = pl.ds(8, 64)
    load_u = pltpu.make_async_copy(interior, pad1.at[pl.ds(1, 2), core], load_sem.at[0])
    load_c = pltpu.make_async_copy(cells, cell_v, load_sem.at[1])
    load_s = pltpu.make_async_copy(sources, src, load_sem.at[2])
    load_a = pltpu.make_async_copy(absorption, inv, load_sem.at[3])
    load_u.start()
    load_c.start()
    inc_loads = []
    for part in range(4):
        rows = pl.ds(part * 1024, 1024)
        inc_loads.append(pltpu.make_async_copy(incident.at[rows], inc_v.at[rows], inc_sem.at[part]))
        inc_loads[-1].start()

    partners = [(slab, lax.rem(blk + k, 8)) for k in range(1, 8)]
    partners += [toward(d) for d in (XA, XB, YA, YB, "z")]
    partners += [(up, blk), (down, blk), (up, east), (up, west), (down, east), (down, west)]
    barrier = pltpu.get_barrier_semaphore()
    for partner in partners:
        pl.semaphore_signal(barrier, inc=1, device_id=partner, device_id_type=MESH)

    panel_loads = []
    for q in (3, 2, 1, 0):
        for r in (3, 2, 1, 0):
            y = flip(my_y, q % 2, r % 2)
            x = flip(my_x, q // 2, r // 2)
            rows = pl.ds(pl.multiple_of(y * 256 + x * 64, 64), 64)
            panel_loads.append(pltpu.make_async_copy(bem.at[rows], panel.at[q, r], panel_sem.at[q, r]))
            panel_loads[-1].start()
    load_s.start()
    load_a.start()

    load_u.wait()
    load_c.wait()
    for z in range(2):
        for c in range(4):
            lanes = pl.ds(c * 128, 128)
            ytx1[0, pl.ds(z * 4 + c, 1), :] = pad1[1 + z, pl.ds(8, 1), lanes]
            ytx1[1, pl.ds(z * 4 + c, 1), :] = pad1[1 + z, pl.ds(71, 1), lanes]
    y_index = lax.broadcasted_iota(jnp.int32, (64, 128), 0) * 2
    for c in range(4):
        cell = cell_v[pl.ds(blk * 4 + c, 1), :]
        total = jnp.zeros((64, 128), F32)
        for z in range(2):
            for side in range(2):
                face = pad1[1 + z, pl.ds(8, 64), pl.ds(511 * side, 1)]
                total += jnp.where(cell == y_index + (z * 128 + side), face, 0.0)
        ttx[pl.ds(c, 1), :] = jnp.sum(total, axis=0, keepdims=True)
    ttx[pl.ds(4, 4), :] = jnp.zeros((4, 128), F32)
    trx[0] = ttx[...]

    pl.semaphore_wait(barrier, len(partners))

    traces = []
    for k in range(1, 8):
        traces.append(pltpu.make_async_remote_copy(
            src_ref=ttx, dst_ref=trx.at[k], send_sem=trace_send.at[k], recv_sem=trace_recv.at[k],
            device_id=(slab, lax.rem(blk + k, 8)), device_id_type=MESH))
        traces[-1].start()

    def halo_copies(sweep, pad, ytx, yrx):
        def copy(n, source, target, device):
            return pltpu.make_async_remote_copy(
                src_ref=source, dst_ref=target, send_sem=halo_send.at[sweep, n],
                recv_sem=halo_recv.at[sweep, n], device_id=device, device_id_type=MESH)
        return [
            copy(0, pad.at[2, core], pad.at[0, core], (up, blk)),
            copy(1, pad.at[1, core], pad.at[3, core], (down, blk)),
            copy(2, ytx.at[1], yrx.at[0], (slab, east)),
            copy(3, ytx.at[1], yrx.at[1], (up, east)),
            copy(4, ytx.at[1], yrx.at[2], (down, east)),
            copy(5, ytx.at[0], yrx.at[3], (slab, west)),
            copy(6, ytx.at[0], yrx.at[4], (up, west)),
            copy(7, ytx.at[0], yrx.at[5], (down, west)),
        ]

    halos1 = halo_copies(0, pad1, ytx1, yrx1)
    halos2 = halo_copies(1, pad2, ytx2, yrx2)
    for copy in halos1:
        copy.start()

    for copy in traces:
        copy.wait_recv()
    turned = jnp.concatenate([trx[...].reshape(64, 128), jnp.zeros((64, 128), F32)], axis=0).T
    for copy in inc_loads:
        copy.wait()
    for k in range(8):
        base = lax.rem(blk + 8 - k, 8) * 512
        for c in range(4):
            rows = pl.ds(pl.multiple_of(base + c * 128, 128), 128)
            column = lax.slice(turned, (0, k * 8 + c), (128, k * 8 + c + 1))
            fld[rows, :] = (inc_v[rows, :].astype(F32) + column).astype(BF16)

    wanted = offset[0] // 4096 + blk // 4
    hit = jnp.full((8, 128), wanted, jnp.int32) == jnp.full((8, 128), slab, jnp.int32)
    coef = jnp.where(hit, 0.5, 0.0).astype(F32)[0:1, 0:1]
    jump_base = lax.rem(blk, 4) * 1024

    boxes = (rx1, rx2, rx3, rx4)

    def rs_copy(part, stage, chunk):
        size = 512 >> stage
        half = size // 2
        start = 0 if chunk == 1 else half
        return pltpu.make_async_remote_copy(
            src_ref=prod.at[part, pl.ds(size + start, half)],
            dst_ref=boxes[stage].at[part, pl.ds(start, half)],
            send_sem=rs_send.at[part, stage, chunk], recv_sem=rs_recv.at[part, stage, chunk],
            device_id=toward(ORDERS[part][stage]), device_id_type=MESH)

    copies = {(p, s, c): rs_copy(p, s, c) for p in range(4) for s in range(4) for c in range(2)}

    for n, copy in enumerate(panel_loads):
        copy.wait()

    def swapped(q):
        return (q % 2) * 2 + q // 2

    def unit(pair, q):
        lhs = panel[q] if pair == 0 else panel[:, q]
        cols = pl.ds(pair * 256, 256)
        out = jnp.dot(lhs.reshape(256, 4096), fld[:, cols], preferred_element_type=F32)
        for r in range(4):
            qa, qb = (q, r) if pair == 0 else (r, q)
            y = flip(my_y, qa % 2, qb % 2)
            x = flip(my_x, qa // 2, qb // 2)
            rows = pl.ds(pl.multiple_of(jump_base + y * 256 + x * 64, 64), 64)
            piece = out[r * 64:(r + 1) * 64] + coef * fld[rows, cols].astype(F32)
            prod[pair * 2, pl.ds(q * 256 + r * 64, 64), :] = piece[:, :128]
            prod[pair * 2 + 1, pl.ds(swapped(q) * 256 + swapped(r) * 64, 64), :] = piece[:, 128:]

    for pair in range(2):
        unit(pair, 3)
        copies[pair * 2, 0, 0].start()
        copies[pair * 2 + 1, 0, 0].start()
    for pair in range(2):
        unit(pair, 2)
        copies[pair * 2, 0, 1].start()
    for pair in range(2):
        unit(pair, 1)
        copies[pair * 2 + 1, 0, 1].start()
    for pair in range(2):
        unit(pair, 0)

    def add_squares(n, total):
        x = fld[pl.ds(pl.multiple_of(n * 128, 128), 128), :].astype(F32)
        return total + jnp.sum((x * x).reshape(16, 8, 512), axis=0)

    ntx[0] = lax.fori_loop(0, 32, add_squares, jnp.zeros((8, 512), F32))
    norm_copies = [
        pltpu.make_async_remote_copy(
            src_ref=ntx.at[s], dst_ref=nrx.at[s], send_sem=n_send.at[s], recv_sem=n_recv.at[s],
            device_id=toward(d), device_id_type=MESH)
        for s, d in enumerate((XA, YA, XB, YB, "z"))
    ]
    norm_copies[0].start()

    load_s.wait()
    load_a.wait()
    inv[...] = 0.6 / (CENTER + inv[...])
    lane = lax.broadcasted_iota(jnp.int32, (64, 512), 1)
    first, last = lane == 0, lane == 511
    keep_down = jnp.where(slab > 0, 1.0, 0.0).astype(F32)
    keep_up = jnp.where(slab < 31, 1.0, 0.0).astype(F32)
    keep_west = jnp.where(blk > 0, 1.0, 0.0).astype(F32)
    keep_east = jnp.where(blk < 7, 1.0, 0.0).astype(F32)

    def sweep(pad, yrx, halos, store):
        for copy in halos:
            copy.wait_recv()
        for c in range(4):
            lanes = pl.ds(c * 128, 128)
            for row, base, keep in ((7, 0, keep_west), (72, 3, keep_east)):
                one = pl.ds(row, 1)
                pad[0, one, lanes] = yrx[base + 1, pl.ds(4 + c, 1), :] * keep
                pad[1, one, lanes] = yrx[base, pl.ds(c, 1), :] * keep
                pad[2, one, lanes] = yrx[base, pl.ds(4 + c, 1), :] * keep
                pad[3, one, lanes] = yrx[base + 2, pl.ds(c, 1), :] * keep

        def beside(z):
            v = pad[z, pl.ds(8, 64), :]
            s = pad[z, pl.ds(7, 64), :] + pad[z, pl.ds(9, 64), :]
            across = s * (1.0 / 6.0) + along_x(v * (1.0 / 6.0) + s * (1.0 / 12.0), first, last)
            return v, s, across

        low = beside(0)[2] * keep_down
        v0, s0, q0 = beside(1)
        v1, s1, q1 = beside(2)
        high = beside(3)[2] * keep_up
        e0 = low + q1 + along_x(s0, first, last) * (1.0 / 6.0)
        e1 = q0 + high + along_x(s1, first, last) * (1.0 / 6.0)
        store(0, 0.4 * v0 + inv[0] * (src[0] + e0))
        store(1, 0.4 * v1 + inv[1] * (src[1] + e1))

    def store_first(z, value):
        pad2[1 + z, pl.ds(8, 64), :] = value

    def store_second(z, value):
        relaxed[z] = value

    sweep(pad1, yrx1, halos1, store_first)
    for z in range(2):
        for c in range(4):
            lanes = pl.ds(c * 128, 128)
            ytx2[0, pl.ds(z * 4 + c, 1), :] = pad2[1 + z, pl.ds(8, 1), lanes]
            ytx2[1, pl.ds(z * 4 + c, 1), :] = pad2[1 + z, pl.ds(71, 1), lanes]
    for copy in halos2:
        copy.start()

    def add_in(part, stage, start, size):
        rows = pl.ds(start, size)
        prod[part, rows, :] += boxes[stage][part, rows, :]

    def norm_step(s):
        norm_copies[s].wait_recv()
        ntx[s + 1] = ntx[s] + nrx[s]
        norm_copies[s + 1].start()

    z_copies = [
        pltpu.make_async_remote_copy(
            src_ref=prod.at[part, pl.ds(pl.multiple_of((1 - my_z) * 32, 32), 32)], dst_ref=rx5.at[part],
            send_sem=rs_send.at[part, 4, 0], recv_sem=rs_recv.at[part, 4, 0],
            device_id=toward("z"), device_id_type=MESH)
        for part in range(4)
    ]

    for stage in range(1, 5):
        width = 1024 >> stage
        half = width // 2
        quarter = half // 2
        for part in range(4):
            copies[part, stage - 1, 0].wait_recv()
            if stage < 4:
                add_in(part, stage - 1, half + quarter, quarter)
                copies[part, stage, 0].start()
                add_in(part, stage - 1, half, quarter)
                copies[part, stage, 1].start()
            else:
                add_in(part, stage - 1, half, half)
        for part in range(4):
            copies[part, stage - 1, 1].wait_recv()
            add_in(part, stage - 1, 0, half)
            if stage == 4:
                z_copies[part].start()
        norm_step(stage - 1)
        if stage == 2:
            sweep(pad2, yrx2, halos2, store_second)

    norm_copies[4].wait_recv()
    sums = jnp.sum(ntx[4] + nrx[4], axis=0, keepdims=True)
    scale = 1.0 / jnp.sqrt(sums / NODES + 1e-06)
    own = pl.ds(pl.multiple_of(my_z * 32, 32), 32)
    for part in range(4):
        lanes = pl.ds(part * 128, 128)
        z_copies[part].wait_recv()
        flux[:, lanes] = (prod[part, own, :] + rx5[part]) * scale[:, part * 128:(part + 1) * 128]

    for copy in traces + halos1 + halos2 + norm_copies + z_copies + list(copies.values()):
        copy.wait_send()


def per_device(interior, sources, absorption, bem_panel, incident, node_cell, offset):
    any_space = pl.BlockSpec(memory_space=pl.ANY)
    vmem = pl.BlockSpec(memory_space=pltpu.VMEM)
    dma = pltpu.SemaphoreType.DMA
    return pl.pallas_call(
        kernel,
        out_shape=(
            jax.ShapeDtypeStruct((2, 64, 512), F32),
            jax.ShapeDtypeStruct((32, 512), F32),
        ),
        in_specs=[pl.BlockSpec(memory_space=pltpu.SMEM)] + [any_space] * 6,
        out_specs=(vmem, vmem),
        scratch_shapes=[
            pltpu.VMEM((4, 80, 512), F32),
            pltpu.VMEM((4, 80, 512), F32),
            pltpu.VMEM((2, 64, 512), F32),
            pltpu.VMEM((2, 64, 512), F32),
            pltpu.VMEM((2, 8, 128), F32),
            pltpu.VMEM((2, 8, 128), F32),
            pltpu.VMEM((6, 8, 128), F32),
            pltpu.VMEM((6, 8, 128), F32),
            pltpu.VMEM((32, 128), jnp.int32),
            pltpu.VMEM((8, 128), F32),
            pltpu.VMEM((8, 8, 128), F32),
            pltpu.VMEM((4096, 512), BF16),
            pltpu.VMEM((4096, 512), BF16),
            pltpu.VMEM((4, 4, 64, 4096), BF16),
            pltpu.VMEM((4, 1024, 128), F32),
            pltpu.VMEM((4, 512, 128), F32),
            pltpu.VMEM((4, 256, 128), F32),
            pltpu.VMEM((4, 128, 128), F32),
            pltpu.VMEM((4, 64, 128), F32),
            pltpu.VMEM((4, 32, 128), F32),
            pltpu.VMEM((5, 8, 512), F32),
            pltpu.VMEM((5, 8, 512), F32),
            dma((4,)),
            dma((4,)),
            dma((4, 4)),
            dma((2, 8)),
            dma((2, 8)),
            dma((8,)),
            dma((8,)),
            dma((4, 5, 2)),
            dma((4, 5, 2)),
            dma((5,)),
            dma((5,)),
        ],
        compiler_params=pltpu.CompilerParams(
            collective_id=0, has_side_effects=True, vmem_limit_bytes=56 * 1024 * 1024
        ),
        cost_estimate=pl.CostEstimate(flops=4300000000, bytes_accessed=14000000, transcendentals=0),
    )(offset, interior, sources, absorption, bem_panel, incident, node_cell.reshape(32, 128))


def solution(mesh):
    in_specs = (
        P("slab", "blk", None),
        P("slab", "blk", None),
        P("slab", "blk", None),
        P("blk", "slab"),
        P("slab", None),
        P("slab"),
        P(),
    )
    out_specs = (P("slab", "blk", None), P(("blk", "slab"), None))
    return jax.shard_map(
        per_device, mesh=mesh, in_specs=in_specs, out_specs=out_specs, check_vma=False
    )
```

time: 480 us -> 51.3 us (0.11)
  the two profiles are of different devices: /device:TPU:2 before, /device:TPU:6 now
where the time goes in v1:
time: 51.3 us; the launch traced here: 51.1 us
  Pallas kernels  46.7 us (91%)
  local copies, waits for them, and re-layouts  3.14 us (6%)
  between operations  1.29 us (3%)
    pallas_call x1, Pallas kernels, per_device(): pl.pallas_call(kernel, out_shape=(jax.ShapeDtypeStruct((2, 64, 512), F32)...  46.7 us
    unnamed x2, local copies, waits for them, and re-layouts  3.14 us

profile of v1, /device:TPU:6, one launch (start us, length us, event | category | flops | bytes accessed | tf_op | source)
XLA Modules:
  0.0 51.1 jit_solution(15770400477817319708)
XLA Ops:
  1.3 46.7 %shard_map.86 = (f32[2,64,512]{2,1,0:T(8,128)}, f32[32,512]{1,0:T(8,128)}) custom-call(s32[1]{0:T(128)S(6)} %copy.11.offset, f32[2,64,512]{2,1,0:T(8,128)} %interior.1, f32[2,64,512]{2,1,0:T(8,128)} %sources.1, f32[2,64,512]{2,1,0:T(8,128)} %absorption.1, bf16[1024,4096]{1,0:T(8,128)(2,1)} %bem.1, bf16[4096,512]{1,0:T(8,128)(2,1)} %incident.1, s32[32,128]{1,0:T(8,128)} %bitcast.1), custom_call_target="tpu_custom_call" | custom-call | flops 4300000256 | bytes 14000000 | tf_op jit(solution)/shard_map/pallas_call | solution.py:324
  47.9 1.7 %copy.12 = f32[2,64,512]{2,1,0:T(8,128)} copy(f32[2,64,512]{2,1,0:T(8,128)} %get-tuple-element.4) | data formatting | bytes 524288
  49.6 1.5 %copy.13 = f32[32,512]{1,0:T(8,128)} copy(f32[32,512]{1,0:T(8,128)} %get-tuple-element.5) | data formatting | bytes 131072

commit v2 on v1

v2 whole, which is shorter than its diff:
```python
import jax
import jax.numpy as jnp
from jax import lax
from jax.experimental import pallas as pl
from jax.experimental.pallas import tpu as pltpu
from jax.sharding import PartitionSpec as P

F32 = jnp.float32
BF16 = jnp.bfloat16
MESH = pl.DeviceIdType.MESH
CENTER = 8.0 / 3.0


def flip(pos, low, high):
    if low:
        pos = pos + 1 - 2 * lax.rem(pos, 2)
    if high:
        pos = 3 - pos
    return pos


XA, XB, YA, YB = ("x", 1, 0), ("x", 0, 1), ("y", 1, 0), ("y", 0, 1)
XAB, YAB = ("x", 1, 1), ("y", 1, 1)
ORDERS = ((XA, YA, XB, YB), (YA, XA, YB, XB), (XB, YB, XA, YA), (YB, XB, YA, XA))
NODES = 131072.0


def along_x(w, first, last):
    n = w.shape[1]
    left = jnp.where(first, 0.0, pltpu.roll(w, 1, 1))
    right = jnp.where(last, 0.0, pltpu.roll(w, n - 1, 1))
    return left + right


def kernel(
    offset, interior, sources, absorption, bem, incident, cells,
    relaxed, flux,
    pad1, pad2, src, inv, ytx1, ytx2, yrx1, yrx2,
    cell_v, ttx, trx, pieces, inc_v, panel,
    prod, rx1, rx2, rx3, rx4, rx5, mtx, mrx,
    load_sem, inc_sem, panel_sem, halo_send, halo_recv,
    trace_send, trace_recv, rs_send, rs_recv, m_send, m_recv,
):
    slab, blk = lax.axis_index("slab"), lax.axis_index("blk")
    my_y, my_x, my_z = slab // 8, lax.rem(slab // 2, 4), lax.rem(slab, 2)

    def at(y, x, z):
        return y * 8 + x * 2 + z

    def toward(dim):
        if dim == "z":
            return (at(my_y, my_x, 1 - my_z), blk)
        axis, low, high = dim
        if axis == "x":
            return (at(my_y, flip(my_x, low, high), my_z), blk)
        return (at(flip(my_y, low, high), my_x, my_z), blk)

    up, down = lax.rem(slab + 1, 32), lax.rem(slab + 31, 32)
    east, west = lax.rem(blk + 1, 8), lax.rem(blk + 7, 8)

    core = pl.ds(8, 64)
    load_u = pltpu.make_async_copy(interior, pad1.at[pl.ds(1, 2), core], load_sem.at[0])
    load_c = pltpu.make_async_copy(cells, cell_v, load_sem.at[1])
    load_s = pltpu.make_async_copy(sources, src, load_sem.at[2])
    load_a = pltpu.make_async_copy(absorption, inv, load_sem.at[3])
    inc_load = pltpu.make_async_copy(incident, inc_v, inc_sem.at[0])
    panel_loads = {}
    order = sorted(((q, r) for q in range(4) for r in range(4)), key=lambda g: (-max(g), -g[0], -g[1]))
    for q, r in order:
        y = flip(my_y, q % 2, r % 2)
        x = flip(my_x, q // 2, r // 2)
        rows = pl.ds(pl.multiple_of(y * 256 + x * 64, 64), 64)
        panel_loads[q, r] = pltpu.make_async_copy(bem.at[rows], panel.at[q, r], panel_sem.at[q, r])
    load_u.start()
    load_c.start()
    inc_load.start()
    for group in order[:4]:
        panel_loads[group].start()

    partners = [(slab, lax.rem(blk + k, 8)) for k in range(1, 8)]
    partners += [toward(d) for d in (XA, XB, XAB, YA, YB, YAB, "z")]
    partners += [(up, blk), (down, blk), (up, east), (up, west), (down, east), (down, west)]
    barrier = pltpu.get_barrier_semaphore()
    for partner in partners:
        pl.semaphore_signal(barrier, inc=1, device_id=partner, device_id_type=MESH)

    load_u.wait()
    for z in range(2):
        for c in range(4):
            lanes = pl.ds(c * 128, 128)
            ytx1[0, pl.ds(z * 4 + c, 1), :] = pad1[1 + z, pl.ds(8, 1), lanes]
            ytx1[1, pl.ds(z * 4 + c, 1), :] = pad1[1 + z, pl.ds(71, 1), lanes]

    def halo_copies(sweep, pad, ytx, yrx):
        def copy(n, source, target, device):
            return pltpu.make_async_remote_copy(
                src_ref=source, dst_ref=target, send_sem=halo_send.at[sweep, n],
                recv_sem=halo_recv.at[sweep, n], device_id=device, device_id_type=MESH)
        return [
            copy(0, pad.at[2, core], pad.at[0, core], (up, blk)),
            copy(1, pad.at[1, core], pad.at[3, core], (down, blk)),
            copy(2, ytx.at[1], yrx.at[0], (slab, east)),
            copy(3, ytx.at[1], yrx.at[1], (up, east)),
            copy(4, ytx.at[1], yrx.at[2], (down, east)),
            copy(5, ytx.at[0], yrx.at[3], (slab, west)),
            copy(6, ytx.at[0], yrx.at[4], (up, west)),
            copy(7, ytx.at[0], yrx.at[5], (down, west)),
        ]

    halos1 = halo_copies(0, pad1, ytx1, yrx1)
    halos2 = halo_copies(1, pad2, ytx2, yrx2)
    pl.semaphore_wait(barrier, len(partners))
    for copy in halos1:
        copy.start()

    for group in order[4:]:
        panel_loads[group].start()
    load_s.start()
    load_a.start()

    load_c.wait()
    y_index = lax.broadcasted_iota(jnp.int32, (64, 128), 0) * 2
    totals = [jnp.zeros((64, 128), F32)] * 4
    for z in range(2):
        for side in range(2):
            face = jnp.broadcast_to(pad1[1 + z, pl.ds(8, 64), pl.ds(511 * side, 1)], (64, 128))
            for c in range(4):
                cell = cell_v[pl.ds(blk * 4 + c, 1), :]
                totals[c] += jnp.where(cell == y_index + (z * 128 + side), face, 0.0)
    found = [jnp.sum(total, axis=0, keepdims=True) for total in totals]
    for c in range(4):
        ttx[pl.ds(c, 1), :] = found[c]

    inc_load.wait()
    turned = jnp.concatenate(found + [jnp.zeros((124, 128), F32)], axis=0).T
    squares = jnp.zeros((8, 512), F32)
    for c in range(4):
        rows = pl.ds(pl.multiple_of(blk * 512 + c * 128, 128), 128)
        column = lax.slice(turned, (0, c), (128, c + 1))
        x = (inc_v[rows, :].astype(F32) + column).astype(BF16).astype(F32)
        squares += jnp.sum((x * x).reshape(16, 8, 512), axis=0)
    squares = jnp.sum(squares, axis=0, keepdims=True)
    for c in range(4):
        ttx[pl.ds(4 + c, 1), :] = squares[:, c * 128:(c + 1) * 128]
    trx[0] = ttx[...]

    traces = []
    for k in range(1, 8):
        traces.append(pltpu.make_async_remote_copy(
            src_ref=ttx, dst_ref=trx.at[k], send_sem=trace_send.at[k], recv_sem=trace_recv.at[k],
            device_id=(slab, lax.rem(blk + k, 8)), device_id_type=MESH))
        traces[-1].start()

    wanted = offset[0] // 4096 + blk // 4
    hit = jnp.full((8, 128), wanted, jnp.int32) == jnp.full((8, 128), slab, jnp.int32)
    coef = jnp.where(hit, 0.5, 0.0).astype(F32)[0:1, 0:1]
    jump_base = lax.rem(blk, 4) * 1024

    boxes = (rx1, rx2, rx3, rx4)
    chunks = (2, 2, 2, 1)
    waited = set()

    def arrived(part, stage, chunk):
        if chunk < chunks[stage] and (part, stage, chunk) not in waited:
            waited.add((part, stage, chunk))
            copies[part, stage, chunk].wait_recv()

    def rs_copy(part, stage, chunk):
        size = 512 >> stage
        piece = size // chunks[stage]
        start = size - (chunk + 1) * piece
        return pltpu.make_async_remote_copy(
            src_ref=prod.at[part, pl.ds(size + start, piece)],
            dst_ref=boxes[stage].at[part, pl.ds(start, piece)],
            send_sem=rs_send.at[part, stage, chunk], recv_sem=rs_recv.at[part, stage, chunk],
            device_id=toward(ORDERS[part][stage]), device_id_type=MESH)

    copies = {(p, s, c): rs_copy(p, s, c) for p in range(4) for s in range(4) for c in range(chunks[s])}

    def swapped(q):
        return (q % 2) * 2 + q // 2

    def unit(pair, q):
        for r in range(4):
            copy = panel_loads.pop((q, r) if pair == 0 else (r, q), None)
            if copy is not None:
                copy.wait()
        lhs = panel[q] if pair == 0 else panel[:, q]
        cols = pl.ds(pair * 256, 256)
        out = jnp.dot(lhs.reshape(256, 4096), inc_v[:, cols], preferred_element_type=F32)
        for r in range(4):
            qa, qb = (q, r) if pair == 0 else (r, q)
            y = flip(my_y, qa % 2, qb % 2)
            x = flip(my_x, qa // 2, qb // 2)
            rows = pl.ds(pl.multiple_of(jump_base + y * 256 + x * 64, 64), 64)
            piece = out[r * 64:(r + 1) * 64] + coef * inc_v[rows, cols].astype(F32)
            prod[pair * 2, pl.ds(q * 256 + r * 64, 64), :] = piece[:, :128]
            prod[pair * 2 + 1, pl.ds(swapped(q) * 256 + swapped(r) * 64, 64), :] = piece[:, 128:]

    for pair in range(2):
        unit(pair, 3)
        copies[pair * 2, 0, 0].start()
        copies[pair * 2 + 1, 0, 0].start()
    for pair in range(2):
        unit(pair, 2)
        copies[pair * 2, 0, 1].start()
    for pair in range(2):
        unit(pair, 1)
        copies[pair * 2 + 1, 0, 1].start()
    for pair in range(2):
        unit(pair, 0)

    lane = lax.broadcasted_iota(jnp.int32, (64, 512), 1)
    first, last = lane == 0, lane == 511
    keep_down = jnp.where(slab > 0, 1.0, 0.0).astype(F32)
    keep_up = jnp.where(slab < 31, 1.0, 0.0).astype(F32)
    keep_west = jnp.where(blk > 0, 1.0, 0.0).astype(F32)
    keep_east = jnp.where(blk < 7, 1.0, 0.0).astype(F32)

    def sweep(pad, yrx, halos, store):
        for copy in halos:
            copy.wait_recv()
        for c in range(4):
            lanes = pl.ds(c * 128, 128)
            for row, base, keep in ((7, 0, keep_west), (72, 3, keep_east)):
                one = pl.ds(row, 1)
                pad[0, one, lanes] = yrx[base + 1, pl.ds(4 + c, 1), :] * keep
                pad[1, one, lanes] = yrx[base, pl.ds(c, 1), :] * keep
                pad[2, one, lanes] = yrx[base, pl.ds(4 + c, 1), :] * keep
                pad[3, one, lanes] = yrx[base + 2, pl.ds(c, 1), :] * keep

        def beside(z):
            v = pad[z, pl.ds(8, 64), :]
            s = pad[z, pl.ds(7, 64), :] + pad[z, pl.ds(9, 64), :]
            across = s * (1.0 / 6.0) + along_x(v * (1.0 / 6.0) + s * (1.0 / 12.0), first, last)
            return v, s, across

        low = beside(0)[2] * keep_down
        v0, s0, q0 = beside(1)
        v1, s1, q1 = beside(2)
        high = beside(3)[2] * keep_up
        e0 = low + q1 + along_x(s0, first, last) * (1.0 / 6.0)
        e1 = q0 + high + along_x(s1, first, last) * (1.0 / 6.0)
        store(0, 0.4 * v0 + inv[0] * (src[0] + e0))
        store(1, 0.4 * v1 + inv[1] * (src[1] + e1))

    def sweep_first():
        load_s.wait()
        load_a.wait()
        inv[...] = 0.6 / (CENTER + inv[...])

        def store(z, value):
            pad2[1 + z, pl.ds(8, 64), :] = value

        sweep(pad1, yrx1, halos1, store)
        for z in range(2):
            for c in range(4):
                lanes = pl.ds(c * 128, 128)
                ytx2[0, pl.ds(z * 4 + c, 1), :] = pad2[1 + z, pl.ds(8, 1), lanes]
                ytx2[1, pl.ds(z * 4 + c, 1), :] = pad2[1 + z, pl.ds(71, 1), lanes]
        for copy in halos2:
            copy.start()

    def sweep_second():
        def store(z, value):
            relaxed[z] = value

        sweep(pad2, yrx2, halos2, store)

    groups = ([XA, XB, XAB], [YA, YB, YAB], ["z"])
    sends = [
        [
            pltpu.make_async_remote_copy(
                src_ref=mtx.at[s], dst_ref=mrx.at[s, n], send_sem=m_send.at[s, n], recv_sem=m_recv.at[s, n],
                device_id=toward(d), device_id_type=MESH)
            for n, d in enumerate(group)
        ]
        for s, group in enumerate(groups)
    ]

    def trace_products():
        for copy in traces:
            copy.wait_recv()
        pieces[...] = jnp.zeros((16, 4096), F32)
        squares = trx[0, pl.ds(4, 4), :]
        for k in range(1, 8):
            squares += trx[k, pl.ds(4, 4), :]
        for k in range(8):
            base = lax.rem(blk + 8 - k, 8) * 512
            for c in range(4):
                lanes = pl.ds(pl.multiple_of(base + c * 128, 128), 128)
                rest = trx[k, pl.ds(c, 1), :]
                for n in range(3):
                    piece = rest.astype(BF16).astype(F32)
                    pieces[pl.ds(n, 1), lanes] = piece
                    rest = rest - piece
        spread = lax.dot_general(
            pieces[...].astype(BF16), panel[...].reshape(1024, 4096), (((1,), (1,)), ((), ())),
            preferred_element_type=F32)
        row = spread[0:1] + spread[1:2] + spread[2:3]
        mtx[0] = jnp.zeros((24, 128), F32)
        mtx[0, pl.ds(0, 4), :] = squares
        for q in range(4):
            for r in range(4):
                y = flip(my_y, q % 2, r % 2)
                x = flip(my_x, q // 2, r // 2)
                g = q * 4 + r
                mtx[0, pl.ds(8 + y * 4 + x, 1), pl.ds(0, 64)] = row[:, g * 64:(g + 1) * 64]
        for g in range(16):
            k = lax.rem(blk + 8 - (lax.rem(blk, 4) * 2 + g // 8), 8)
            there = trx[k, pl.ds(g % 8 // 2, 1), :][:, g % 2 * 64:g % 2 * 64 + 64]
            mtx[0, pl.ds(8 + g, 1), pl.ds(0, 64)] += coef * there
        for copy in sends[0]:
            copy.start()

    def message_sum(s):
        total = mtx[s]
        for n, copy in enumerate(sends[s]):
            copy.wait_recv()
            total += mrx[s, n]
        return total

    def message_step(s):
        mtx[s] = message_sum(s - 1)
        for copy in sends[s]:
            copy.start()

    def added(part, rows, stages):
        total = prod[part, rows, :]
        for stage in range(stages):
            total += boxes[stage][part, rows, :]
        return total

    def halving(stage):
        size = 512 >> stage
        for part in range(4):
            if stage >= 2:
                arrived(part, stage - 2, 1)
            arrived(part, stage - 1, 0)
            piece = size // chunks[stage]
            for chunk in range(chunks[stage]):
                rows = pl.ds(2 * size - (chunk + 1) * piece, piece)
                prod[part, rows, :] = added(part, rows, stage)
                copies[part, stage, chunk].start()

    own = pl.ds(pl.multiple_of(my_z * 32, 32), 32)
    other = pl.ds(pl.multiple_of((1 - my_z) * 32, 32), 32)
    z_copies = [
        pltpu.make_async_remote_copy(
            src_ref=prod.at[part, other], dst_ref=rx5.at[part],
            send_sem=rs_send.at[part, 4, 0], recv_sem=rs_recv.at[part, 4, 0],
            device_id=toward("z"), device_id_type=MESH)
        for part in range(4)
    ]

    def last_halving():
        for part in range(4):
            arrived(part, 2, 1)
            arrived(part, 3, 0)
            arrived(part, 3, 1)
            prod[part, other, :] = added(part, other, 4)
            z_copies[part].start()

    def finish():
        message = message_sum(2)
        mtx[3] = message
        row = mtx[3, pl.ds(8 + my_y * 4 + my_x, 1), :]
        here = lax.broadcasted_iota(jnp.int32, (32, 128), 1) == (
            lax.broadcasted_iota(jnp.int32, (32, 128), 0) + 32 * my_z)
        column = jnp.sum(jnp.where(here, row, 0.0), axis=1, keepdims=True)
        for part in range(4):
            scale = 1.0 / jnp.sqrt(message[part:part + 1] / NODES + 1e-06)
            z_copies[part].wait_recv()
            flux[:, pl.ds(part * 128, 128)] = (added(part, own, 4) + rx5[part] + column) * scale

    halving(1)
    trace_products()
    sweep_first()
    halving(2)
    message_step(1)
    halving(3)
    message_step(2)
    last_halving()
    sweep_second()
    finish()

    for copy in traces + halos1 + halos2 + sum(sends, []) + z_copies + list(copies.values()):
        copy.wait_send()


def hand_over(relaxed, flux, relaxed_out, flux_out):
    relaxed_out[...] = relaxed[...]
    flux_out[...] = flux[...]


def per_device(interior, sources, absorption, bem_panel, incident, node_cell, offset):
    any_space = pl.BlockSpec(memory_space=pl.ANY)
    vmem = pl.BlockSpec(memory_space=pltpu.VMEM)
    dma = pltpu.SemaphoreType.DMA
    shapes = (
        jax.ShapeDtypeStruct((2, 64, 512), F32),
        jax.ShapeDtypeStruct((32, 512), F32),
    )
    results = pl.pallas_call(
        kernel,
        out_shape=shapes,
        in_specs=[pl.BlockSpec(memory_space=pltpu.SMEM)] + [any_space] * 6,
        out_specs=(vmem, vmem),
        scratch_shapes=[
            pltpu.VMEM((4, 80, 512), F32),
            pltpu.VMEM((4, 80, 512), F32),
            pltpu.VMEM((2, 64, 512), F32),
            pltpu.VMEM((2, 64, 512), F32),
            pltpu.VMEM((2, 8, 128), F32),
            pltpu.VMEM((2, 8, 128), F32),
            pltpu.VMEM((6, 8, 128), F32),
            pltpu.VMEM((6, 8, 128), F32),
            pltpu.VMEM((32, 128), jnp.int32),
            pltpu.VMEM((8, 128), F32),
            pltpu.VMEM((8, 8, 128), F32),
            pltpu.VMEM((16, 4096), F32),
            pltpu.VMEM((4096, 512), BF16),
            pltpu.VMEM((4, 4, 64, 4096), BF16),
            pltpu.VMEM((4, 1024, 128), F32),
            pltpu.VMEM((4, 512, 128), F32),
            pltpu.VMEM((4, 256, 128), F32),
            pltpu.VMEM((4, 128, 128), F32),
            pltpu.VMEM((4, 64, 128), F32),
            pltpu.VMEM((4, 32, 128), F32),
            pltpu.VMEM((4, 24, 128), F32),
            pltpu.VMEM((3, 3, 24, 128), F32),
            dma((4,)),
            dma((4,)),
            dma((4, 4)),
            dma((2, 8)),
            dma((2, 8)),
            dma((8,)),
            dma((8,)),
            dma((4, 5, 2)),
            dma((4, 5, 2)),
            dma((3, 3)),
            dma((3, 3)),
        ],
        compiler_params=pltpu.CompilerParams(
            collective_id=0, has_side_effects=True, vmem_limit_bytes=56 * 1024 * 1024
        ),
        cost_estimate=pl.CostEstimate(flops=4300000000, bytes_accessed=14000000, transcendentals=0),
    )(offset, interior, sources, absorption, bem_panel, incident, node_cell.reshape(32, 128))
    return pl.pallas_call(
        hand_over,
        out_shape=shapes,
        in_specs=[vmem] * 2,
        out_specs=(vmem,) * 2,
    )(*results)


def solution(mesh):
    in_specs = (
        P("slab", "blk", None),
        P("slab", "blk", None),
        P("slab", "blk", None),
        P("blk", "slab"),
        P("slab", None),
        P("slab"),
        P(),
    )
    out_specs = (P("slab", "blk", None), P(("blk", "slab"), None))
    return jax.shard_map(
        per_device, mesh=mesh, in_specs=in_specs, out_specs=out_specs, check_vma=False
    )
```

time: 51.3 us -> 41.7 us (0.81)
  the two profiles are of different devices: /device:TPU:6 before, /device:TPU:2 now
where the time goes in v2:
time: 41.7 us; the launch traced here: 41.6 us
  Pallas kernels  40.3 us (97%)
  between operations  1.29 us (3%)
    pallas_call x1, Pallas kernels, per_device(): pl.pallas_call(kernel, out_shape=shapes, in_specs=[pl.BlockSpec(memory_sp...  38.7 us
    pallas_call x1, Pallas kernels, per_device(): pl.pallas_call(hand_over, out_shape=shapes, in_specs=[vmem] * 2, out_spec...  1.69 us

profile of v2, /device:TPU:2, one launch (start us, length us, event | category | flops | bytes accessed | tf_op | source)
XLA Modules:
  0.0 41.6 jit_solution(7959430966701525309)
XLA Ops:
  1.3 38.7 %shard_map.86 = (f32[2,64,512]{2,1,0:T(8,128)}, f32[32,512]{1,0:T(8,128)}) custom-call(s32[1]{0:T(128)S(6)} %copy.9.offset, f32[2,64,512]{2,1,0:T(8,128)} %interior.1, f32[2,64,512]{2,1,0:T(8,128)} %sources.1, f32[2,64,512]{2,1,0:T(8,128)} %absorption.1, bf16[1024,4096]{1,0:T(8,128)(2,1)} %bem.1, bf16[4096,512]{1,0:T(8,128)(2,1)} %incident.1, s32[32,128]{1,0:T(8,128)} %bitcast.1), custom_call_target="tpu_custom_call" | custom-call | flops 4300000256 | bytes 14000000 | tf_op jit(solution)/shard_map/pallas_call | solution.py:404
  39.9 1.7 %shard_map.87 = (f32[2,64,512]{2,1,0:T(8,128)}, f32[32,512]{1,0:T(8,128)}) custom-call(f32[2,64,512]{2,1,0:T(8,128)} %get-tuple-element.4.relaxed, f32[32,512]{1,0:T(8,128)} %get-tuple-element.5.flux), custom_call_target="tpu_custom_call" | custom-call | tf_op jit(solution)/shard_map/pallas_call | solution.py:449

commit v3 on v2

--- a/solution.py
+++ b/solution.py
@@ -34,11 +34,11 @@
 
 def kernel(
     offset, interior, sources, absorption, bem, incident, cells,
-    relaxed, flux,
+    relaxed_out, flux_out, relaxed, flux,
     pad1, pad2, src, inv, ytx1, ytx2, yrx1, yrx2,
     cell_v, ttx, trx, pieces, inc_v, panel,
     prod, rx1, rx2, rx3, rx4, rx5, mtx, mrx,
-    load_sem, inc_sem, panel_sem, halo_send, halo_recv,
+    out_sem, load_sem, inc_sem, panel_sem, halo_send, halo_recv,
     trace_send, trace_recv, rs_send, rs_recv, m_send, m_recv,
 ):
     slab, blk = lax.axis_index("slab"), lax.axis_index("blk")
@@ -110,46 +110,24 @@
     halos1 = halo_copies(0, pad1, ytx1, yrx1)
     halos2 = halo_copies(1, pad2, ytx2, yrx2)
     pl.semaphore_wait(barrier, len(partners))
-    for copy in halos1:
+    def start_planes(halos, near):
+        @pl.when(my_z == (0 if near else 1))
+        def _():
+            halos[0].start()
+
+        @pl.when(my_z == (1 if near else 0))
+        def _():
+            halos[1].start()
+
+    for copy in halos1[2:]:
         copy.start()
+    start_planes(halos1, False)
+    start_planes(halos1, True)
 
     for group in order[4:]:
         panel_loads[group].start()
     load_s.start()
     load_a.start()
-
-    load_c.wait()
-    y_index = lax.broadcasted_iota(jnp.int32, (64, 128), 0) * 2
-    totals = [jnp.zeros((64, 128), F32)] * 4
-    for z in range(2):
-        for side in range(2):
-            face = jnp.broadcast_to(pad1[1 + z, pl.ds(8, 64), pl.ds(511 * side, 1)], (64, 128))
-            for c in range(4):
-                cell = cell_v[pl.ds(blk * 4 + c, 1), :]
-                totals[c] += jnp.where(cell == y_index + (z * 128 + side), face, 0.0)
-    found = [jnp.sum(total, axis=0, keepdims=True) for total in totals]
-    for c in range(4):
-        ttx[pl.ds(c, 1), :] = found[c]
-
-    inc_load.wait()
-    turned = jnp.concatenate(found + [jnp.zeros((124, 128), F32)], axis=0).T
-    squares = jnp.zeros((8, 512), F32)
-    for c in range(4):
-        rows = pl.ds(pl.multiple_of(blk * 512 + c * 128, 128), 128)
-        column = lax.slice(turned, (0, c), (128, c + 1))
-        x = (inc_v[rows, :].astype(F32) + column).astype(BF16).astype(F32)
-        squares += jnp.sum((x * x).reshape(16, 8, 512), axis=0)
-    squares = jnp.sum(squares, axis=0, keepdims=True)
-    for c in range(4):
-        ttx[pl.ds(4 + c, 1), :] = squares[:, c * 128:(c + 1) * 128]
-    trx[0] = ttx[...]
-
-    traces = []
-    for k in range(1, 8):
-        traces.append(pltpu.make_async_remote_copy(
-            src_ref=ttx, dst_ref=trx.at[k], send_sem=trace_send.at[k], recv_sem=trace_recv.at[k],
-            device_id=(slab, lax.rem(blk + k, 8)), device_id_type=MESH))
-        traces[-1].start()
 
     wanted = offset[0] // 4096 + blk // 4
     hit = jnp.full((8, 128), wanted, jnp.int32) == jnp.full((8, 128), slab, jnp.int32)
@@ -197,10 +175,46 @@
             prod[pair * 2, pl.ds(q * 256 + r * 64, 64), :] = piece[:, :128]
             prod[pair * 2 + 1, pl.ds(swapped(q) * 256 + swapped(r) * 64, 64), :] = piece[:, 128:]
 
-    for pair in range(2):
+    def first_units(pair):
         unit(pair, 3)
         copies[pair * 2, 0, 0].start()
         copies[pair * 2 + 1, 0, 0].start()
+
+    load_c.wait()
+    y_index = lax.broadcasted_iota(jnp.int32, (64, 128), 0) * 2
+    totals = [jnp.zeros((64, 128), F32)] * 4
+    for z in range(2):
+        for side in range(2):
+            face = jnp.broadcast_to(pad1[1 + z, pl.ds(8, 64), pl.ds(511 * side, 1)], (64, 128))
+            for c in range(4):
+                cell = cell_v[pl.ds(blk * 4 + c, 1), :]
+                totals[c] += jnp.where(cell == y_index + (z * 128 + side), face, 0.0)
+    found = [jnp.sum(total, axis=0, keepdims=True) for total in totals]
+    for c in range(4):
+        ttx[pl.ds(c, 1), :] = found[c]
+
+    inc_load.wait()
+    turned = jnp.concatenate(found + [jnp.zeros((124, 128), F32)], axis=0).T
+    squares = jnp.zeros((8, 512), F32)
+    for c in range(4):
+        rows = pl.ds(pl.multiple_of(blk * 512 + c * 128, 128), 128)
+        column = lax.slice(turned, (0, c), (128, c + 1))
+        x = (inc_v[rows, :].astype(F32) + column).astype(BF16).astype(F32)
+        squares += jnp.sum((x * x).reshape(16, 8, 512), axis=0)
+    squares = jnp.sum(squares, axis=0, keepdims=True)
+    for c in range(4):
+        ttx[pl.ds(4 + c, 1), :] = squares[:, c * 128:(c + 1) * 128]
+    trx[0] = ttx[...]
+
+    traces = []
+    for k in range(1, 8):
+        traces.append(pltpu.make_async_remote_copy(
+            src_ref=ttx, dst_ref=trx.at[k], send_sem=trace_send.at[k], recv_sem=trace_recv.at[k],
+            device_id=(slab, lax.rem(blk + k, 8)), device_id_type=MESH))
+        traces[-1].start()
+
+    for pair in range(2):
+        first_units(pair)
     for pair in range(2):
         unit(pair, 2)
         copies[pair * 2, 0, 1].start()
@@ -258,14 +272,20 @@
                 lanes = pl.ds(c * 128, 128)
                 ytx2[0, pl.ds(z * 4 + c, 1), :] = pad2[1 + z, pl.ds(8, 1), lanes]
                 ytx2[1, pl.ds(z * 4 + c, 1), :] = pad2[1 + z, pl.ds(71, 1), lanes]
-        for copy in halos2:
+        for copy in halos2[2:]:
             copy.start()
+        start_planes(halos2, False)
+        start_planes(halos2, True)
+
+    relaxed_copy = pltpu.make_async_copy(relaxed, relaxed_out, out_sem.at[0])
+    flux_copy = pltpu.make_async_copy(flux, flux_out, out_sem.at[1])
 
     def sweep_second():
         def store(z, value):
             relaxed[z] = value
 
         sweep(pad2, yrx2, halos2, store)
+        relaxed_copy.start()
 
     groups = ([XA, XB, XAB], [YA, YB, YAB], ["z"])
     sends = [
@@ -372,20 +392,32 @@
             scale = 1.0 / jnp.sqrt(message[part:part + 1] / NODES + 1e-06)
             z_copies[part].wait_recv()
             flux[:, pl.ds(part * 128, 128)] = (added(part, own, 4) + rx5[part] + column) * scale
+        flux_copy.start()
+
+    def sent(group):
+        for copy in group:
+            copy.wait_send()
+
+    def stage_copies(stage):
+        return [copies[p, stage, c] for p in range(4) for c in range(chunks[stage])]
 
     halving(1)
     trace_products()
     sweep_first()
     halving(2)
+    sent(traces + halos1 + stage_copies(0))
     message_step(1)
     halving(3)
+    sent(sends[0] + stage_copies(1))
     message_step(2)
     last_halving()
+    sent(sends[1] + halos2 + stage_copies(2))
     sweep_second()
     finish()
 
-    for copy in traces + halos1 + halos2 + sum(sends, []) + z_copies + list(copies.values()):
-        copy.wait_send()
+    sent(sends[2] + stage_copies(3) + z_copies)
+    relaxed_copy.wait()
+    flux_copy.wait()
 
 
 def hand_over(relaxed, flux, relaxed_out, flux_out):
@@ -405,8 +437,10 @@
         kernel,
         out_shape=shapes,
         in_specs=[pl.BlockSpec(memory_space=pltpu.SMEM)] + [any_space] * 6,
-        out_specs=(vmem, vmem),
+        out_specs=(any_space, any_space),
         scratch_shapes=[
+            pltpu.VMEM((2, 64, 512), F32),
+            pltpu.VMEM((32, 512), F32),
             pltpu.VMEM((4, 80, 512), F32),
             pltpu.VMEM((4, 80, 512), F32),
             pltpu.VMEM((2, 64, 512), F32),
@@ -429,6 +463,7 @@
             pltpu.VMEM((4, 32, 128), F32),
             pltpu.VMEM((4, 24, 128), F32),
             pltpu.VMEM((3, 3, 24, 128), F32),
+            dma((2,)),
             dma((4,)),
             dma((4,)),
             dma((4, 4)),

time: 41.7 us -> 40.3 us (0.966)
  Pallas kernels: 40.3 us -> 39 us
    pallas_call x1, Pallas kernels: 38.7 us -> 37.3 us  [per_device(): pl.pallas_call(kernel, out_shape=shapes, in_specs=[pl.BlockSpec(memory_sp...]
where the time goes in v3:
time: 40.3 us; the launch traced here: 40.2 us
  Pallas kernels  39 us (97%)
  between operations  1.29 us (3%)
    pallas_call x1, Pallas kernels, per_device(): pl.pallas_call(kernel, out_shape=shapes, in_specs=[pl.BlockSpec(memory_sp...  37.3 us
    pallas_call x1, Pallas kernels, per_device(): pl.pallas_call(hand_over, out_shape=shapes, in_specs=[vmem] * 2, out_spec...  1.69 us

profile of v3, /device:TPU:2, one launch (start us, length us, event | category | flops | bytes accessed | tf_op | source)
XLA Modules:
  0.0 40.2 jit_solution(6858868817400650660)
XLA Ops:
  1.3 37.3 %shard_map.86 = (f32[2,64,512]{2,1,0:T(8,128)}, f32[32,512]{1,0:T(8,128)}) custom-call(s32[1]{0:T(128)S(6)} %copy.9.offset, f32[2,64,512]{2,1,0:T(8,128)} %interior.1, f32[2,64,512]{2,1,0:T(8,128)} %sources.1, f32[2,64,512]{2,1,0:T(8,128)} %absorption.1, bf16[1024,4096]{1,0:T(8,128)(2,1)} %bem.1, bf16[4096,512]{1,0:T(8,128)(2,1)} %incident.1, s32[32,128]{1,0:T(8,128)} %bitcast.1), custom_call_target="tpu_custom_call" | custom-call | flops 4300000256 | bytes 14000000 | tf_op jit(solution)/shard_map/pallas_call | solution.py:436
  38.6 1.7 %shard_map.87 = (f32[2,64,512]{2,1,0:T(8,128)}, f32[32,512]{1,0:T(8,128)}) custom-call(f32[2,64,512]{2,1,0:T(8,128)} %get-tuple-element.4.relaxed, f32[32,512]{1,0:T(8,128)} %get-tuple-element.5.flux), custom_call_target="tpu_custom_call" | custom-call | tf_op jit(solution)/shard_map/pallas_call | solution.py:484

commit v4 on v3

--- a/solution.py
+++ b/solution.py
@@ -409,8 +409,8 @@
     message_step(1)
     halving(3)
     sent(sends[0] + stage_copies(1))
+    last_halving()
     message_step(2)
-    last_halving()
     sent(sends[1] + halos2 + stage_copies(2))
     sweep_second()
     finish()

time: 40.3 us -> 40.6 us (level)
  no operation moved by 1% of the time
where the time goes in v4:
time: 40.6 us; the launch traced here: 40.5 us
  Pallas kernels  39.2 us (97%)
  between operations  1.29 us (3%)
    pallas_call x1, Pallas kernels, per_device(): pl.pallas_call(kernel, out_shape=shapes, in_specs=[pl.BlockSpec(memory_sp...  37.5 us
    pallas_call x1, Pallas kernels, per_device(): pl.pallas_call(hand_over, out_shape=shapes, in_specs=[vmem] * 2, out_spec...  1.69 us

profile of v4, /device:TPU:2, one launch (start us, length us, event | category | flops | bytes accessed | tf_op | source)
XLA Modules:
  0.0 40.5 jit_solution(2656038780808713482)
XLA Ops:
  1.3 37.5 %shard_map.86 = (f32[2,64,512]{2,1,0:T(8,128)}, f32[32,512]{1,0:T(8,128)}) custom-call(s32[1]{0:T(128)S(6)} %copy.9.offset, f32[2,64,512]{2,1,0:T(8,128)} %interior.1, f32[2,64,512]{2,1,0:T(8,128)} %sources.1, f32[2,64,512]{2,1,0:T(8,128)} %absorption.1, bf16[1024,4096]{1,0:T(8,128)(2,1)} %bem.1, bf16[4096,512]{1,0:T(8,128)(2,1)} %incident.1, s32[32,128]{1,0:T(8,128)} %bitcast.1), custom_call_target="tpu_custom_call" | custom-call | flops 4300000256 | bytes 14000000 | tf_op jit(solution)/shard_map/pallas_call | solution.py:436
  38.8 1.7 %shard_map.87 = (f32[2,64,512]{2,1,0:T(8,128)}, f32[32,512]{1,0:T(8,128)}) custom-call(f32[2,64,512]{2,1,0:T(8,128)} %get-tuple-element.4.relaxed, f32[32,512]{1,0:T(8,128)} %get-tuple-element.5.flux), custom_call_target="tpu_custom_call" | custom-call | tf_op jit(solution)/shard_map/pallas_call | solution.py:484
